TPU v7x, 32 devices: a whole 2x2x4 slice. The times are simulated.
32 devices in a mesh: bank: 16 (over z, y, x), tm: 2 (over core).
Axes of the slice: x: 2, y: 2, z: 4, core: 2. Of those that a mesh axis runs over, the one named last changes fastest.
Arguments:
- raw_strain: float32 [3, 2, 2048], P(None, 'tm', 'bank'), may hold values from -6 to 6
- psd_scale: float32 [3, 2, 16], P(None, 'tm', 'bank'), may hold values from 0.25 to 8
- basis_filters: bfloat16 [16, 128, 128], P('bank'), may hold values from -0.5 to 0.5
- recon_matrix: bfloat16 [16, 128, 2, 768], P('bank', None, None, 'tm'), may hold values from -0.5 to 0.5
- bin_taps: int32 [16], P('bank'), may hold values from 32 to 128, as said below
- bin_band: int32 [16], P('bank'), may hold values from 0 to 2, as said below
- bin_window: int32 [16], P('bank'), may hold values from 0 to 7
- window_start: int32 [8], replicated, may hold values from 512 to 1536, as said below
Outputs:
- peak_snr: float32 [3, 12288], P(None, ('bank', 'tm'))
- mean_power: float32 [3, 12288], P(None, ('bank', 'tm'))
- loudest: float32 [3, 4096], P(None, 'tm')
Inputs may be any that keep to these rules, and one draw needn't show every extreme that they name: `bin_taps`: some bin uses 128 taps and some the fewest. `bin_band`: the lowest and the highest band each occur. `window_start`: a window starts at each end of the range.
All inputs are finite; a program needn't handle non-finite values.
Results may differ from a plain program's by a relative error of at most 0.0035.
Values may be sent and summed in bfloat16 or wider, within the bound.
A program may use at most 64 MiB of HBM per device.

v0:
```python
import jax
import jax.numpy as jnp
from jax import lax
from jax.sharding import PartitionSpec as P

epsilon = 1e-06


def from_behind(block, axis, distance):
    devices = range(lax.axis_size(axis))
    route = [(i - distance, i) for i in devices if i - distance in devices]
    return lax.ppermute(block, axis, route)


def as_sent(shard):

    def short(part):
        return part.astype(jnp.bfloat16) if part.dtype == jnp.float32 else part

    return jax.tree.map(short, shard)


def averaged_series(lengthened_series, decimation_ratio):
    zero_extended = jnp.concatenate(
        [
            jnp.zeros((lengthened_series.shape[0], 3), jnp.float32),
            lengthened_series.astype(jnp.float32),
        ],
        axis=1,
    )
    extent_total = lengthened_series.shape[1]
    accumulated_total = jnp.zeros((lengthened_series.shape[0], extent_total), jnp.float32)
    for delayed_series in range(4):
        accumulated_total = accumulated_total + jnp.where(
            delayed_series < decimation_ratio,
            zero_extended[:, 3 - delayed_series : 3 - delayed_series + extent_total],
            jnp.float32(0.0),
        )
    return (accumulated_total / decimation_ratio.astype(jnp.float32)).astype(jnp.bfloat16)


def filter_segment(gentle_average, basis_filters, bin_taps, frequency_level, seg_len, reach):
    taps_max = basis_filters.shape[1]
    kernel_coefficient_slot = jnp.arange(taps_max, dtype=jnp.int32)
    masked_basis = (
        basis_filters[0] * (kernel_coefficient_slot < bin_taps[0]).astype(jnp.bfloat16)[:, None]
    )
    kernel = masked_basis[::-1][:, None, :]

    def make_branch(rate):
        first = reach - rate * (taps_max - 1)
        span = seg_len + rate * (taps_max - 1)

        def run_branch(signal):
            inputs = signal[:, first : first + span][:, :, None]
            result = lax.conv_general_dilated(
                inputs,
                kernel,
                (1,),
                "VALID",
                rhs_dilation=(rate,),
                dimension_numbers=("NHC", "HIO", "NHC"),
                preferred_element_type=jnp.float32,
            )
            return result.astype(jnp.bfloat16)

        return run_branch

    return lax.switch(
        jnp.clip(frequency_level, 0, 2),
        [make_branch(1), make_branch(2), make_branch(4)],
        gentle_average,
    )


def template_stats(filtered, recon_mat, first_instant, interval_opening_reading, interval_extent):
    detectors, row_count, feature_count = filtered.shape
    tpl_count = recon_mat.shape[1] // 2
    tile_line_total = min(512, row_count)
    block_count = row_count // tile_line_total
    blocks = filtered.reshape(detectors * block_count, tile_line_total, feature_count)
    offsets = (
        jnp.arange(detectors * block_count, dtype=jnp.int32) % block_count * tile_line_total
        + first_instant
    )

    def one_block(paired):
        rows_block, displacement_table = paired
        result_moments = displacement_table + jnp.arange(tile_line_total, dtype=jnp.int32)
        inside_limits = (result_moments >= interval_opening_reading) & (
            result_moments < interval_opening_reading + interval_extent
        )
        complex_snr = jnp.dot(rows_block, recon_mat, preferred_element_type=jnp.float32)
        powers = complex_snr[:, :tpl_count] ** 2 + complex_snr[:, tpl_count:] ** 2
        masked = jnp.where(inside_limits[:, None], powers, jnp.float32(0.0))
        return (jnp.max(masked, axis=0), jnp.sum(masked, axis=0), jnp.max(masked, axis=1))

    peaks, totals, series = lax.map(one_block, (blocks, offsets))
    peak_found = jnp.max(peaks.reshape(detectors, block_count, tpl_count), axis=1)
    total_found = jnp.sum(totals.reshape(detectors, block_count, tpl_count), axis=1)
    return (peak_found, total_found, series.reshape(detectors, row_count))


def per_device(
    raw_strain, psd_scale, basis_filters, recon_matrix, bin_taps, bin_band, bin_window, window_start
):
    seg_index = lax.axis_index("tm")
    tm_count = lax.axis_size("tm")
    scaled = raw_strain * psd_scale
    segment = lax.all_gather(scaled, "bank", axis=2, tiled=True)[:, 0, :]
    seg_len = segment.shape[1]
    detector_readings = seg_len * tm_count
    squares = lax.psum(jnp.sum(scaled * scaled, axis=(1, 2)), ("bank", "tm"))
    norm_scale = jnp.sqrt(squares / detector_readings + epsilon)
    whitened = (segment / norm_scale[:, None]).astype(jnp.bfloat16)
    reach = 4 * basis_filters.shape[1]
    history = from_behind(whitened[:, seg_len - reach :], "tm", 1)
    lengthened_series = jnp.concatenate([history, whitened], axis=1)
    frequency_level = bin_band[0]
    decimation_ratio = jnp.where(
        frequency_level == 0, 1, jnp.where(frequency_level == 1, 2, 4)
    ).astype(jnp.int32)
    gentle_average = averaged_series(lengthened_series, decimation_ratio)
    filtered = filter_segment(
        gentle_average, basis_filters, bin_taps, frequency_level, seg_len, reach
    )
    interval_opening_reading = jnp.sum(
        jnp.where(
            jnp.arange(window_start.shape[0], dtype=jnp.int32) == bin_window[0], window_start, 0
        )
    )
    tpl_count = recon_matrix.shape[3]
    feature_count = recon_matrix.shape[1]
    whole = jax.tree.map(
        lambda part, own: part.astype(own.dtype),
        lax.all_gather(as_sent(filtered), "tm", axis=1, tiled=True),
        filtered,
    )
    recon_mat = recon_matrix[0].reshape(feature_count, 2 * tpl_count)
    peak_snr, totals, series = template_stats(
        whole, recon_mat, 0, interval_opening_reading, seg_len
    )
    loud_series = lax.pmax(series, ("bank", "tm"))
    loudest = lax.dynamic_slice_in_dim(loud_series, seg_index * seg_len, seg_len, 1)
    return (peak_snr, totals / seg_len, loudest)


def solution(mesh):
    return jax.shard_map(
        per_device,
        mesh=mesh,
        in_specs=(
            P(None, "tm", "bank"),
            P(None, "tm", "bank"),
            P("bank", None, None),
            P("bank", None, None, "tm"),
            P("bank"),
            P("bank"),
            P("bank"),
            P(),
        ),
        out_specs=(P(None, ("bank", "tm")), P(None, ("bank", "tm")), P(None, "tm")),
        check_vma=False,
    )
```

profile of v0, /device:TPU:0, one launch (start us, length us, event | category | flops | bytes accessed | tf_op | source)
XLA Modules:
  0.0 289.6 jit_solution(3737400440321451287)
XLA Ops:
  8.1 42.5 %all_gather.6 = f32[3,1,2048]{2,0,1:T(4,128)S(1)} all-gather(f32[3,1,128]{2,0,1:T(4,128)S(1)} %get-tuple-element.143), channel_id=1, replica_groups=mesh['bank'=16,'tm'=2] {'bank'}, dimensions={2}, use_global_device_ids=true | all-gather | bytes 26112 | tf_op jit(solution)/shard_map/all_gather | solution.py:110
  50.6 36.8 %psum.7 = f32[3]{0:T(128)S(1)} all-reduce(f32[3]{0:T(128)S(1)} %get-tuple-element.142), channel_id=1, replica_groups=mesh['bank'=16,'tm'=2] {'bank','tm'}, use_global_device_ids=true, to_apply=%region_1.0 | all-reduce | flops 3 | bytes 24 | tf_op jit(solution)/shard_map/psum | solution.py:113
  87.6 1.3 collective-permute-start
  91.2 10.1 %conditional.2 = (bf16[3,2048,128]{2,1,0:T(8,128)(2,1)S(1)}) conditional(s32[]{:T(128)} %bitcast.11, (bf16[3,2560]{1,0:T(4,128)(2,1)S(1)}, bf16[128,1,128]{2,0,1:T(8,128)(2,1)S(1)}) %tuple.61, (bf16[3,2560]{1,0:T(4,128)(2,1)S(1)}, bf16[128,1,128]{2,0,1:T(8,128)(2,1)S(1)}) %tuple.62, (bf16[3,2560]{1,0:T(4,128)(2,1)S(1)}, ...), branch_computations={%region_2.3_spmd, %region_3.4_spmd, %region_4.5_spmd} | conditional | flops 227455200 | bytes 8726634
  91.7 9.0 %convolution_select_fusion = bf16[24,272,128]{2,0,1:T(8,128)(2,1)S(1)} fusion(bf16[24,399,1]{0,2,1:T(2,128)(2,1)S(1)} %copy.19, pred[24,272]{0,1:T(8,128)(4,1)} %constant.107, bf16[128,1,128]{2,0,1:T(8,128)(2,1)S(1)} %get-tuple-element.116), kind=kOutput, calls=%fused_computation | convolution fusion | flops 214745088 | bytes 1729616 | tf_op jit(solution)/shard_map/cond/branch_0_fun/conv_general_dilated | solution.py:56
  104.5 50.8 %all-gather.2.cloned.1.call-done = bf16[3,4096,128]{2,1,0:T(8,128)(2,1)} async-done(((bf16[3,2048,128]{2,1,0:T(8,128)(2,1)}), bf16[3,4096,128]{2,1,0:T(8,128)(2,1)}) %all-gather.2.cloned.1.call-update) | async-done | bytes 3145744 | tf_op jit(solution)/shard_map/all_gather | solution.py:136
  155.3 84.7 %while.15 = (s32[]{:T(128)}, f32[24,384]{1,0:T(8,128)S(1)}, f32[24,384]{1,0:T(8,128)S(1)}, f32[24,512]{1,0:T(8,128)S(1)}, s32[24]{0:T(128)S(1)}, /*index=5*/s32[...) while((s32[]{:T(128)}, f32[24,384]{1,0:T(8,128)S(1)}, ...), condition=%wide.region_10.11_spmd, body=%wide.region_6.10_spmd.sunk | while | flops 102040320 | bytes 3496593 | solution.py:98
  155.9 1.2 fusion.36
  157.1 1.3 fusion.35
  159.4 1.2 fusion.36
  160.6 1.3 fusion.35
  162.9 1.2 fusion.36
  164.1 1.3 fusion.35
  166.5 1.2 fusion.36
  167.7 1.3 fusion.35
  170.0 1.2 fusion.36
  171.2 1.3 fusion.35
  173.5 1.2 fusion.36
  174.7 1.3 fusion.35
  177.0 1.2 fusion.36
  178.2 1.3 fusion.35
  180.6 1.2 fusion.36
  181.8 1.3 fusion.35
  184.1 1.2 fusion.36
  185.3 1.3 fusion.35
  187.6 1.2 fusion.36
  188.8 1.3 fusion.35
  191.2 1.2 fusion.36
  192.4 1.3 fusion.35
  195.9 1.3 fusion.35
  199.4 1.3 fusion.35
  202.9 1.3 fusion.35
  206.5 1.3 fusion.35
  210.0 1.3 fusion.35
  213.5 1.3 fusion.35
  217.1 1.3 fusion.35
  220.6 1.3 fusion.35
  222.9 1.2 fusion.36
  224.1 1.3 fusion.35
  226.4 1.2 fusion.36
  227.6 1.3 fusion.35
  230.0 1.2 fusion.36
  231.2 1.3 fusion.35
  233.5 1.2 fusion.36
  234.7 1.3 fusion.35
  237.0 1.2 fusion.36
  238.2 1.3 fusion.35
  241.3 40.9 %pmax.7 = f32[3,4096]{1,0:T(4,128)S(1)} all-reduce(f32[3,4096]{1,0:T(4,128)S(1)} %reshape.61), channel_id=1, replica_groups=mesh['bank'=16,'tm'=2] {'bank','tm'}, use_global_device_ids=true, to_apply=%region_13.14 | all-reduce | flops 12288 | bytes 98304 | tf_op jit(solution)/shard_map/pmax | solution.py:143
  (212 shorter events, 40.4 us)
Async XLA Ops:
  7.2 148.2 %all-gather.2.cloned.1.call-start = ((), (), s32[]{:S(2)}) async-start(), calls=%async_computation | async-start | bytes 4718592 | tf_op jit(solution)/shard_map/all_gather | solution.py:136
  87.6 3.5 %collective-permute-start = (bf16[3,512]{1,0:T(4,128)(2,1)S(1)}, bf16[3,512]{1,0:T(4,128)(2,1)S(1)}, u32[]{:S(2)}, u32[]{:S(2)}) collective-permute-start(bf16[3,512]{1,0:T(4,128)(2,1)S(1)} %slice.43), channel_id=1, source_target_pairs={{0,1},{2,3},{4,5},{6,7},{8,9},{10,11},{12,13},{14,15},{16,17},{18,... | collective-permute-start | bytes 9224 | tf_op jit(solution)/shard_map/ppermute | solution.py:12
  101.3 1.1 copy-start
  101.3 1.8 copy-start.1
  101.4 1.9 copy-start.2
Sparse Core Ops, SparseCore 0:
  102.6 52.6 all-gather.1
where the time goes:
time: 291 us; the launch traced here: 290 us
  blocking collectives  120 us (41%)
  waiting for transfers between devices  50.8 us (17%)
  other arithmetic  39.4 us (14%)
  matrix products  39.1 us (13%)
  local copies, waits for them, and re-layouts  20 us (7%)
  between operations  16.8 us (6%)
    all_gather x1, waiting for transfers between devices, per_device(): lax.all_gather(as_sent(filtered), 'tm', axis=1, tiled=True)  50.8 us
    all_gather x1, blocking collectives, per_device(): segment = lax.all_gather(scaled, 'bank', axis=2, tiled=True)[:, 0, :]  42.5 us
    pmax x1, blocking collectives, per_device(): loud_series = lax.pmax(series, ('bank', 'tm'))  40.9 us
    psum x1, blocking collectives, per_device(): squares = lax.psum(jnp.sum(scaled * scaled, axis=(1, 2)), ('bank', 'tm'))  36.8 us
    dot_general x24, matrix products, one_block(): jnp.dot(rows_block, recon_mat, preferred_element_type=jnp.float32)  30.1 us
    and x24, other arithmetic, one_block(): (result_moments >= interval_opening_reading) & (result_moments < interval...  28.6 us
    dynamic_slice x24, local copies, waits for them, and re-layouts, template_stats(): peaks, totals, series = lax.map(one_block, (blocks, offsets))  13.3 us
    conv_general_dilated x1, matrix products, run_branch(): lax.conv_general_dilated(inputs, kernel, (1,), 'VALID', rhs_dilation=(rat...  9.02 us
  transfers between devices with their start and end apart: 2, of which 1 were waited for; matrix products, arithmetic and copies ran while one was open for 1% of the time, Pallas kernels for 0%

commit v1 on v0

v1 whole, which is shorter than its diff:
```python
import functools

import jax
import jax.numpy as jnp
from jax import lax
from jax.experimental import pallas as pl
from jax.experimental.pallas import tpu as pltpu
from jax.sharding import PartitionSpec as P

EPSILON = 1e-06
LANES = 128
SEG_CHUNKS = 16
CHUNKS = 32
WIN = 2048
FIRST = 4
LAST = 28
STEPS = 9
REL = 2 * STEPS
PAD = 8
DET = 3
SLOT = 4
MESH = pl.DeviceIdType.MESH


def wait_bytes(ref, sem):
    pltpu.make_async_copy(ref, ref, sem).wait()


def fold_filters(basis_ref, recon_ref, taps, gains):
    features = basis_ref.shape[2]
    tap = lax.broadcasted_iota(jnp.int32, basis_ref.shape[1:], 0)
    basis = jnp.where(tap < taps, basis_ref[0].astype(jnp.float32), 0.0).astype(jnp.bfloat16)
    row = lax.broadcasted_iota(jnp.int32, (features, 2 * features), 0)
    col = lax.broadcasted_iota(jnp.int32, (features, 2 * features), 1)
    pairs = recon_ref[0].reshape(2 * features, recon_ref.shape[3])
    for c in range(2):
        spread = jnp.where(col == 2 * row + c, 1.0, 0.0).astype(jnp.bfloat16)
        wide = jnp.dot(basis, spread, preferred_element_type=jnp.float32).astype(jnp.bfloat16)
        g = jnp.dot(wide, pairs, preferred_element_type=jnp.float32)
        gt = g.T.astype(jnp.bfloat16)
        gains[:, 8 * c : 8 * c + 8, :] = gt.reshape(-1, 8, gt.shape[1])


def whiten_and_smooth(strain, d, rate, smooth):
    x = strain[:, d, :]
    ss = jnp.sum(jnp.sum(x * x, axis=0, keepdims=True), axis=1, keepdims=True)
    norm = jnp.sqrt(ss / (CHUNKS * LANES) + EPSILON)
    w = (x / norm).astype(jnp.bfloat16).astype(jnp.float32)
    lane = lax.broadcasted_iota(jnp.int32, w.shape, 1)
    row = lax.broadcasted_iota(jnp.int32, w.shape, 0)
    before = jnp.where(row == 0, 0.0, pltpu.roll(w, 1, 0))
    total = w
    for j in range(1, 4):
        late = jnp.where(lane < j, pltpu.roll(before, j, 1), pltpu.roll(w, j, 1))
        total = total + jnp.where(j < rate, late, 0.0)
    mean = total / rate.astype(jnp.float32)
    smooth[d] = mean.astype(jnp.bfloat16).astype(jnp.float32)


def lay_delays(d, rate, start, smooth, octet):
    count = REL + 4
    y = jnp.broadcast_to(smooth[d, pl.ds(start - 4, count), :][:, None, :], (count, 8, LANES))
    lane = lax.broadcasted_iota(jnp.int32, y.shape, 2)
    sub = lax.broadcasted_iota(jnp.int32, y.shape, 1)
    for bit in (1, 2, 4):
        shift = rate * bit
        r = pltpu.roll(y, shift, 2)
        late = jnp.where(lane < shift, jnp.concatenate([r[:1], r[:-1]], axis=0), r)
        y = jnp.where((sub & bit) != 0, late, y)
    octet[d] = y


def lay_taps(h, d, rate, offset, octet, taps_ref):
    lane = lax.broadcasted_iota(jnp.int32, (REL, 8, LANES), 2)
    when = lax.broadcasted_iota(jnp.int32, (REL, 8, LANES), 0) * LANES + lane
    inside = (when >= offset) & (when < offset + WIN)
    halves = []
    for e in range(2):
        eights = rate * (2 * h + e)
        back = eights // 16
        shift = 8 * (eights - 16 * back)
        r = pltpu.roll(octet[d, pl.ds(3 - back, REL + 1)], shift, 2)
        halves.append(jnp.where(inside, jnp.where(lane < shift, r[:-1], r[1:]), 0.0))
    both = jnp.concatenate(halves, axis=1).astype(jnp.bfloat16)
    at = pl.ds(pl.multiple_of(16 * h, 16), 16)
    for i in range(REL):
        taps_ref[d, at, LANES * i : LANES * (i + 1)] = both[i]


def score_pair(p, taps_ref, gains, peak, total, series):
    weights = gains[...]
    weights = weights.reshape(-1, weights.shape[2])
    for d in range(DET):
        at = pl.ds(pl.multiple_of(2 * LANES * p, 2 * LANES), 2 * LANES)
        snr = jnp.dot(weights, taps_ref[d, :, at], preferred_element_type=jnp.float32)
        snr = snr.reshape(-1, 2, 8, 2 * LANES)
        re, im = snr[:, 0], snr[:, 1]
        power = re * re + im * im
        left, right = power[:, :, :LANES], power[:, :, LANES:]
        peak[d] = jnp.maximum(peak[d], jnp.maximum(left, right))
        total[d] = total[d] + (left + right)
        loud = jnp.max(jnp.max(power, axis=0), axis=0, keepdims=True)
        series[PAD + 2 * p, d : d + 1, :] = loud[:, :LANES]
        series[PAD + 2 * p + 1, d : d + 1, :] = loud[:, LANES:]


def finish_templates(peak, total, peak_ref, mean_ref):
    for d in range(DET):
        top = peak[d].reshape(-1, LANES).T
        peak_ref[d : d + 1, :] = jnp.max(top, axis=0, keepdims=True)
        add = total[d].reshape(-1, LANES).T
        mean_ref[d : d + 1, :] = jnp.sum(add, axis=0, keepdims=True) * (1.0 / WIN)


def settings(taps_s, band_s, window_s, start_s):
    band = band_s[0]
    rate = jnp.where(band == 0, 1, jnp.where(band == 1, 2, 4)).astype(jnp.int32)
    opening = jnp.clip(start_s[window_s[0]], FIRST * LANES, LAST * LANES - WIN)
    start = opening // LANES
    return taps_s[0], rate, start, opening - LANES * start


def clear(peak, total, series):
    peak[...] = jnp.zeros_like(peak)
    total[...] = jnp.zeros_like(total)
    series[...] = jnp.zeros_like(series)


def lay_all(strain, rate, start, offset, smooth, octet, taps_ref):
    for d in range(DET):
        whiten_and_smooth(strain, d, rate, smooth)
    for d in range(DET):
        lay_delays(d, rate, start, smooth, octet)

    def body(h, carry):
        for d in range(DET):
            lay_taps(h, d, rate, offset, octet, taps_ref)
        return carry

    lax.fori_loop(0, 8, body, 0)


def local_kernel(
    taps_s, band_s, window_s, start_s, strain, basis_ref, recon_ref,
    peak_ref, mean_ref, loud_ref,
    smooth, octet, taps_ref, gains, peak, total, series,
):
    taps, rate, start, offset = settings(taps_s, band_s, window_s, start_s)
    clear(peak, total, series)
    fold_filters(basis_ref, recon_ref, taps, gains)
    lay_all(strain, rate, start, offset, smooth, octet, taps_ref)
    lax.fori_loop(
        0, STEPS, lambda p, c: (score_pair(p, taps_ref, gains, peak, total, series), c)[1], 0
    )
    loud_ref[...] = jnp.zeros_like(loud_ref)
    for q in range(FIRST, LAST):
        loud_ref[q] = series[PAD + q - start]
    finish_templates(peak, total, peak_ref, mean_ref)


def linked_kernel(
    n_bank,
    taps_s, band_s, window_s, start_s, scale_s, raw_ref, basis_ref, recon_ref,
    peak_ref, mean_ref, loud_ref,
    mine, strain, smooth, octet, taps_ref, gains, peak, total, series,
    parts, found, best, heard,
    gather_out, gather_in, part_out, part_in, best_out, best_in,
):
    bank, tm = lax.axis_index("bank"), lax.axis_index("tm")
    me = tm * n_bank + bank
    others = 2 * n_bank - 1

    def place(q):
        return (lax.rem(q, n_bank), q // n_bank)

    barrier = pltpu.get_barrier_semaphore()

    def greet(i, carry):
        to = place(lax.rem(me + i, 2 * n_bank))
        pl.semaphore_signal(barrier, inc=1, device_id=to, device_id_type=MESH)
        return carry

    lax.fori_loop(1, 2 * n_bank, greet, 0)
    taps, rate, start, offset = settings(taps_s, band_s, window_s, start_s)
    for d in range(DET):
        mine[d : d + 1, :] = raw_ref[d] * scale_s[d, 0, 0]
    mine[DET:SLOT, :] = jnp.zeros((SLOT - DET, LANES), jnp.float32)
    strain[me] = mine[...]
    pl.semaphore_wait(barrier, others)

    def share(i, carry):
        to = place(lax.rem(me + i, 2 * n_bank))
        pltpu.make_async_remote_copy(
            src_ref=mine, dst_ref=strain.at[me], send_sem=gather_out, recv_sem=gather_in,
            device_id=to, device_id_type=MESH,
        ).start()
        return carry

    lax.fori_loop(1, 2 * n_bank, share, 0)
    clear(peak, total, series)
    fold_filters(basis_ref, recon_ref, taps, gains)
    wait_bytes(strain.at[pl.ds(0, others)], gather_in)
    lay_all(strain, rate, start, offset, smooth, octet, taps_ref)
    lax.fori_loop(
        0, STEPS, lambda p, c: (score_pair(p, taps_ref, gains, peak, total, series), c)[1], 0
    )
    for q in range(FIRST, LAST):
        parts[q - FIRST] = series[PAD + q - start]

    owner = (me >= FIRST) & (me < LAST)

    def spread(q, carry):
        @pl.when(q != me)
        def _():
            pltpu.make_async_remote_copy(
                src_ref=parts.at[q - FIRST], dst_ref=found.at[me],
                send_sem=part_out, recv_sem=part_in,
                device_id=place(q), device_id_type=MESH,
            ).start()

        return carry

    lax.fori_loop(FIRST, LAST, spread, 0)

    @pl.when(owner)
    def _():
        found[me] = parts[me - FIRST]
        wait_bytes(found.at[pl.ds(0, others)], part_in)
        best[...] = jnp.max(found[...], axis=0)
        heard[bank] = best[...]

        def announce(i, carry):
            to = (lax.rem(bank + i, n_bank), tm)
            pltpu.make_async_remote_copy(
                src_ref=best, dst_ref=heard.at[bank], send_sem=best_out, recv_sem=best_in,
                device_id=to, device_id_type=MESH,
            ).start()
            return carry

        lax.fori_loop(1, n_bank, announce, 0)

    finish_templates(peak, total, peak_ref, mean_ref)
    wait_bytes(strain.at[pl.ds(0, others)], gather_out)

    @pl.when(owner)
    def _():
        wait_bytes(parts.at[pl.ds(0, LAST - FIRST - 1)], part_out)
        wait_bytes(heard.at[pl.ds(0, SEG_CHUNKS - FIRST - 1)], best_in)
        wait_bytes(heard.at[pl.ds(0, n_bank - 1)], best_out)

    @pl.when(jnp.logical_not(owner))
    def _():
        wait_bytes(parts, part_out)
        wait_bytes(heard.at[pl.ds(0, SEG_CHUNKS - FIRST)], best_in)

    for c in range(n_bank):
        low, high = FIRST, LAST - SEG_CHUNKS
        block = heard[c, 0:DET, :]
        if c < low:
            block = jnp.where(tm == 0, 0.0, block)
        if c >= high:
            block = jnp.where(tm == 1, 0.0, block)
        loud_ref[:, LANES * c : LANES * (c + 1)] = block


def scratch(taps, templates):
    groups = templates // 8
    return [
        pltpu.VMEM((DET, CHUNKS, LANES), jnp.float32),
        pltpu.VMEM((DET, REL + 4, 8, LANES), jnp.float32),
        pltpu.VMEM((DET, taps, REL * LANES), jnp.bfloat16),
        pltpu.VMEM((groups, 16, taps), jnp.bfloat16),
        pltpu.VMEM((DET, groups, 8, LANES), jnp.float32),
        pltpu.VMEM((DET, groups, 8, LANES), jnp.float32),
        pltpu.VMEM((CHUNKS, SLOT, LANES), jnp.float32),
    ]


VMEM = pl.BlockSpec(memory_space=pltpu.VMEM)
SMEM = pl.BlockSpec(memory_space=pltpu.SMEM)
VMEM_LIMIT = 32 * 1024 * 1024


def per_device(
    raw_strain, psd_scale, basis_filters, recon_matrix, bin_taps, bin_band, bin_window, window_start
):
    n_bank, n_tm = lax.axis_size("bank"), lax.axis_size("tm")
    taps, templates = basis_filters.shape[1], recon_matrix.shape[3]
    stats = jax.ShapeDtypeStruct((DET, templates), jnp.float32)
    scalars = (bin_taps, bin_band, bin_window, window_start)
    if raw_strain.shape[2] == LANES and n_bank == SEG_CHUNKS and n_tm == 2:
        slots = pltpu.VMEM((CHUNKS, SLOT, LANES), jnp.float32)
        return pl.pallas_call(
            functools.partial(linked_kernel, n_bank),
            out_shape=(stats, stats, jax.ShapeDtypeStruct((DET, n_bank * LANES), jnp.float32)),
            in_specs=[SMEM] * 5 + [VMEM] * 3,
            out_specs=(VMEM,) * 3,
            scratch_shapes=[pltpu.VMEM((SLOT, LANES), jnp.float32), slots]
            + scratch(taps, templates)
            + [
                pltpu.VMEM((LAST - FIRST, SLOT, LANES), jnp.float32),
                slots,
                pltpu.VMEM((SLOT, LANES), jnp.float32),
                pltpu.VMEM((n_bank, SLOT, LANES), jnp.float32),
            ]
            + [pltpu.SemaphoreType.DMA] * 6,
            compiler_params=pltpu.CompilerParams(
                collective_id=0, has_side_effects=True, vmem_limit_bytes=VMEM_LIMIT
            ),
        )(*scalars, psd_scale, raw_strain, basis_filters, recon_matrix)

    scaled = raw_strain * psd_scale
    whole = lax.all_gather(scaled, "bank", axis=2, tiled=True)
    whole = lax.all_gather(whole, "tm", axis=1, tiled=True)
    blocks = whole.reshape(DET, CHUNKS, LANES).transpose(1, 0, 2)
    blocks = jnp.pad(blocks, ((0, 0), (0, SLOT - DET), (0, 0)))
    peak, mean, loud = pl.pallas_call(
        local_kernel,
        out_shape=(stats, stats, jax.ShapeDtypeStruct((CHUNKS, SLOT, LANES), jnp.float32)),
        in_specs=[SMEM] * 4 + [VMEM] * 3,
        out_specs=(VMEM,) * 3,
        scratch_shapes=scratch(taps, templates),
        compiler_params=pltpu.CompilerParams(vmem_limit_bytes=VMEM_LIMIT),
    )(*scalars, blocks, basis_filters, recon_matrix)
    loud = lax.pmax(loud[:, :DET].transpose(1, 0, 2).reshape(DET, CHUNKS * LANES), ("bank", "tm"))
    length = CHUNKS * LANES // n_tm
    return peak, mean, lax.dynamic_slice_in_dim(loud, lax.axis_index("tm") * length, length, 1)


def solution(mesh):
    return jax.shard_map(
        per_device,
        mesh=mesh,
        in_specs=(
            P(None, "tm", "bank"),
            P(None, "tm", "bank"),
            P("bank", None, None),
            P("bank", None, None, "tm"),
            P("bank"),
            P("bank"),
            P("bank"),
            P(),
        ),
        out_specs=(P(None, ("bank", "tm")), P(None, ("bank", "tm")), P(None, "tm")),
        check_vma=False,
    )
```

time: 291 us -> 32.7 us (0.11)
  blocking collectives: 120 us -> 0 us
  waiting for transfers between devices: 50.8 us -> 0 us
  other arithmetic: 39.4 us -> 0 us
  matrix products: 39.1 us -> 0 us
  Pallas kernels: 0 us -> 25.6 us
  local copies, waits for them, and re-layouts: 20 us -> 4.14 us
  between operations: 16.8 us -> 2.64 us
    all_gather x1 -> x0, waiting for transfers between devices: 50.8 us -> none  [per_device(): lax.all_gather(as_sent(filtered), 'tm', axis=1, tiled=True)]
    all_gather x1 -> x0, blocking collectives: 42.5 us -> none  [per_device(): segment = lax.all_gather(scaled, 'bank', axis=2, tiled=True)[:, 0, :]]
    pmax x1 -> x0, blocking collectives: 40.9 us -> none  [per_device(): loud_series = lax.pmax(series, ('bank', 'tm'))]
    psum x1 -> x0, blocking collectives: 36.8 us -> none  [per_device(): squares = lax.psum(jnp.sum(scaled * scaled, axis=(1, 2)), ('bank', 'tm'))]
    dot_general x24 -> x0, matrix products: 30.1 us -> none  [one_block(): jnp.dot(rows_block, recon_mat, preferred_element_type=jnp.float32)]
    and x24 -> x0, other arithmetic: 28.6 us -> none  [one_block(): (result_moments >= interval_opening_reading) & (result_moments < interval...]
    pallas_call x0 -> x1, Pallas kernels: none -> 25.6 us  [per_device(): pl.pallas_call(functools.partial(linked_kernel, n_bank), out_shape=(stats...]
    dynamic_slice x25 -> x0, local copies, waits for them, and re-layouts: 13.9 us -> none  [the longest x24 13.3 us: template_stats(): peaks, totals, series = lax.map(one_block, (blocks, offsets))]
  transfers between devices with their start and end apart: 2 -> 0, of which waited for: 1 -> 0; matrix products, arithmetic and copies ran while one was open for 1% -> 0% of each run, Pallas kernels for 0% -> 0%
where the time goes in v1:
time: 32.7 us; the launch traced here: 32.4 us
  Pallas kernels  25.6 us (78%)
  local copies, waits for them, and re-layouts  4.14 us (13%)
  between operations  2.64 us (8%)
    pallas_call x1, Pallas kernels, per_device(): pl.pallas_call(functools.partial(linked_kernel, n_bank), out_shape=(stats...  25.6 us
    unnamed x14, local copies, waits for them, and re-layouts  4.14 us

profile of v1, /device:TPU:0, one launch (start us, length us, event | category | flops | bytes accessed | tf_op | source)
XLA Modules:
  0.0 32.4 jit_solution(16076687162145313306)
XLA Ops:
  1.3 0.0 copy-start.4
  1.9 0.0 copy-start.2
  2.6 0.0 copy-done.4
  2.6 0.0 copy-start.3
  2.6 0.1 copy.11.scale_s
  2.7 0.0 copy-done.2
  2.7 0.6 %copy-done.3 = s32[8]{0:T(128)S(1)} copy-done((s32[8]{0:T(128)S(1)}, s32[8]{0:T(128)}, u32[]{:S(2)}) %copy-start.3) | copy-done | bytes 56
  3.3 0.0 copy-start
  3.3 0.9 %copy-done = bf16[1,128,2,384]{3,2,1,0:T(2,128)(2,1)S(1)} copy-done((bf16[1,128,2,384]{3,2,1,0:T(2,128)(2,1)S(1)}, bf16[1,128,2,384]{3,2,1,0:T(2,128)(2,1)}, u32[]{:S(2)}) %copy-start) | copy-done | bytes 196632
  4.2 0.0 copy-start.1
  4.2 0.8 %copy-done.1 = bf16[1,128,128]{2,1,0:T(8,128)(2,1)S(1)} copy-done((bf16[1,128,128]{2,1,0:T(8,128)(2,1)S(1)}, bf16[1,128,128]{2,1,0:T(8,128)(2,1)}, u32[]{:S(2)}) %copy-start.1) | copy-done | bytes 32792
  5.0 25.6 %shard_map.103 = (f32[3,384]{1,0:T(4,128)S(1)}, f32[3,384]{1,0:T(4,128)S(1)}, f32[3,2048]{1,0:T(4,128)S(1)}) custom-call(s32[1]{0:T(128)S(6)} %copy.15.taps_s, s32[1]{0:T(128)S(6)} %copy.16.band_s, s32[1]{0:T(128)S(6)} %copy.17.window_s, s32[8]{0:T(128)S(1)} %copy-done.3, f32[3,1,1]{2,1,0:T(1,128)S(1)} %copy.11.scale_s, f32[3,1,128]{2,1,0:T(1,128)S(1)} %copy-done.2, ...), custom_call_target="tpu_custom_call" | custom-call | tf_op jit(solution)/shard_map/pallas_call | solution.py:293
  30.6 0.6 %copy.18 = f32[3,384]{1,0:T(4,128)} copy(f32[3,384]{1,0:T(4,128)S(1)} %get-tuple-element.6) | data formatting | bytes 9216
  31.2 0.6 %copy.19 = f32[3,384]{1,0:T(4,128)} copy(f32[3,384]{1,0:T(4,128)S(1)} %get-tuple-element.7) | data formatting | bytes 9216
  31.8 0.6 %copy.20 = f32[3,2048]{1,0:T(4,128)} copy(f32[3,2048]{1,0:T(4,128)S(1)} %get-tuple-element.8) | data formatting | bytes 49152
Async XLA Ops:
  1.3 1.3 %copy-start.4 = (f32[3,1,1]{0,2,1:T(1,128)S(1)}, f32[3,1,1]{0,2,1:T(1,128)}, u32[]{:S(2)}) copy-start(f32[3,1,1]{0,2,1:T(1,128)} %param.9) | copy-start | bytes 40
  1.9 0.8 %copy-start.2 = (f32[3,1,128]{2,1,0:T(1,128)S(1)}, f32[3,1,128]{2,1,0:T(1,128)}, u32[]{:S(2)}) copy-start(f32[3,1,128]{2,1,0:T(1,128)} %raw_ref.1) | copy-start | bytes 4612
  2.6 0.7 %copy-start.3 = (s32[8]{0:T(128)S(1)}, s32[8]{0:T(128)}, u32[]{:S(2)}) copy-start(s32[8]{0:T(128)} %start_s.1) | copy-start | bytes 100
  3.3 0.9 %copy-start = (bf16[1,128,2,384]{3,2,1,0:T(2,128)(2,1)S(1)}, bf16[1,128,2,384]{3,2,1,0:T(2,128)(2,1)}, u32[]{:S(2)}) copy-start(bf16[1,128,2,384]{3,2,1,0:T(2,128)(2,1)} %recon_ref.1) | copy-start | bytes 589828
  4.2 0.8 %copy-start.1 = (bf16[1,128,128]{2,1,0:T(8,128)(2,1)S(1)}, bf16[1,128,128]{2,1,0:T(8,128)(2,1)}, u32[]{:S(2)}) copy-start(bf16[1,128,128]{2,1,0:T(8,128)(2,1)} %basis_ref.1) | copy-start | bytes 98308

commit v2 on v1

--- a/solution.py
+++ b/solution.py
@@ -19,6 +19,8 @@
 PAD = 8
 DET = 3
 SLOT = 4
+LINE, PLANE, GROUP = 4, 4, 8
+SHARE = (LAST - FIRST) // GROUP
 MESH = pl.DeviceIdType.MESH
 
 
@@ -159,108 +161,114 @@
 
 
 def linked_kernel(
-    n_bank,
+    taps_h, band_h, window_h, start_h, scale_h, raw_h, basis_h, recon_h,
+    peak_ref, mean_ref, loud_ref,
     taps_s, band_s, window_s, start_s, scale_s, raw_ref, basis_ref, recon_ref,
-    peak_ref, mean_ref, loud_ref,
-    mine, strain, smooth, octet, taps_ref, gains, peak, total, series,
-    parts, found, best, heard,
-    gather_out, gather_in, part_out, part_in, best_out, best_in,
+    strain, ordered, smooth, octet, taps_ref, gains, peak, total, series,
+    parts, found, plane_best, best, heard,
+    fetched, lines_out, lines_in, plane_out, plane_in,
+    part_out, part_in, line_out, line_in, best_out, best_in,
 ):
     bank, tm = lax.axis_index("bank"), lax.axis_index("tm")
-    me = tm * n_bank + bank
-    others = 2 * n_bank - 1
-
-    def place(q):
-        return (lax.rem(q, n_bank), q // n_bank)
-
-    barrier = pltpu.get_barrier_semaphore()
-
-    def greet(i, carry):
-        to = place(lax.rem(me + i, 2 * n_bank))
-        pl.semaphore_signal(barrier, inc=1, device_id=to, device_id_type=MESH)
-        return carry
-
-    lax.fori_loop(1, 2 * n_bank, greet, 0)
-    taps, rate, start, offset = settings(taps_s, band_s, window_s, start_s)
-    for d in range(DET):
-        mine[d : d + 1, :] = raw_ref[d] * scale_s[d, 0, 0]
-    mine[DET:SLOT, :] = jnp.zeros((SLOT - DET, LANES), jnp.float32)
-    strain[me] = mine[...]
-    pl.semaphore_wait(barrier, others)
-
-    def share(i, carry):
-        to = place(lax.rem(me + i, 2 * n_bank))
+    z, xy = bank // PLANE, lax.rem(bank, PLANE)
+    mine = tm * PLANE + xy
+
+    def along(i):
+        return (lax.rem(z + i, LINE) * PLANE + xy, tm)
+
+    def across(g):
+        return (z * PLANE + lax.rem(g, PLANE), g // PLANE)
+
+    def send(src, dst, out, into, to):
         pltpu.make_async_remote_copy(
-            src_ref=mine, dst_ref=strain.at[me], send_sem=gather_out, recv_sem=gather_in,
+            src_ref=src, dst_ref=dst, send_sem=out, recv_sem=into,
             device_id=to, device_id_type=MESH,
         ).start()
+
+    barrier = pltpu.get_barrier_semaphore()
+    for i in range(1, LINE):
+        pl.semaphore_signal(barrier, inc=1, device_id=along(i), device_id_type=MESH)
+    for i in range(1, GROUP):
+        to = across(lax.rem(mine + i, GROUP))
+        pl.semaphore_signal(barrier, inc=1, device_id=to, device_id_type=MESH)
+    pairs = (
+        (scale_h, scale_s), (raw_h, raw_ref), (taps_h, taps_s), (band_h, band_s),
+        (window_h, window_s), (start_h, start_s), (basis_h, basis_ref), (recon_h, recon_ref),
+    )
+    fetches = [pltpu.make_async_copy(a, b, fetched.at[i]) for i, (a, b) in enumerate(pairs)]
+    for fetch in fetches:
+        fetch.start()
+    fetches[0].wait()
+    fetches[1].wait()
+    block = jnp.concatenate([raw_ref[d] * scale_s[d] for d in range(DET)], axis=0)
+    here = mine * LINE + z
+    strain[here] = jnp.concatenate([block, jnp.zeros((SLOT - DET, LANES), jnp.float32)], axis=0)
+    pl.semaphore_wait(barrier, LINE + GROUP - 2)
+    for i in range(1, LINE):
+        send(strain.at[here], strain.at[here], lines_out, lines_in, along(i))
+    clear(peak, total, series)
+    for fetch in fetches[2:]:
+        fetch.wait()
+    taps, rate, start, offset = settings(taps_s, band_s, window_s, start_s)
+    run = strain.at[pl.ds(mine * LINE, LINE)]
+    wait_bytes(strain.at[pl.ds(0, LINE - 1)], lines_in)
+    for i in range(1, GROUP):
+        send(run, run, plane_out, plane_in, across(lax.rem(mine + i, GROUP)))
+    fold_filters(basis_ref, recon_ref, taps, gains)
+    wait_bytes(strain.at[pl.ds(0, (GROUP - 1) * LINE)], plane_in)
+    for q in range(CHUNKS):
+        t, line, spot = q // SEG_CHUNKS, q % SEG_CHUNKS // PLANE, q % PLANE
+        ordered[q] = strain[(t * PLANE + spot) * LINE + line]
+    lay_all(ordered, rate, start, offset, smooth, octet, taps_ref)
+
+    def pass_on(g):
+        for i in range(SHARE):
+            parts[g, i] = series[PAD + FIRST + SHARE * g + i - start]
+
+        @pl.when(mine != g)
+        def _():
+            send(parts.at[g], found.at[mine], part_out, part_in, across(jnp.int32(g)))
+
+    def step(p, carry):
+        score_pair(p, taps_ref, gains, peak, total, series)
+        for g in range(GROUP):
+            due = SHARE * g + SHARE - 1
+            if due < 2 * STEPS - 2:
+                pl.when(p == due // 2)(functools.partial(pass_on, g))
         return carry
 
-    lax.fori_loop(1, 2 * n_bank, share, 0)
-    clear(peak, total, series)
-    fold_filters(basis_ref, recon_ref, taps, gains)
-    wait_bytes(strain.at[pl.ds(0, others)], gather_in)
-    lay_all(strain, rate, start, offset, smooth, octet, taps_ref)
-    lax.fori_loop(
-        0, STEPS, lambda p, c: (score_pair(p, taps_ref, gains, peak, total, series), c)[1], 0
-    )
-    for q in range(FIRST, LAST):
-        parts[q - FIRST] = series[PAD + q - start]
-
-    owner = (me >= FIRST) & (me < LAST)
-
-    def spread(q, carry):
-        @pl.when(q != me)
-        def _():
-            pltpu.make_async_remote_copy(
-                src_ref=parts.at[q - FIRST], dst_ref=found.at[me],
-                send_sem=part_out, recv_sem=part_in,
-                device_id=place(q), device_id_type=MESH,
-            ).start()
-
-        return carry
-
-    lax.fori_loop(FIRST, LAST, spread, 0)
-
-    @pl.when(owner)
-    def _():
-        found[me] = parts[me - FIRST]
-        wait_bytes(found.at[pl.ds(0, others)], part_in)
-        best[...] = jnp.max(found[...], axis=0)
-        heard[bank] = best[...]
-
-        def announce(i, carry):
-            to = (lax.rem(bank + i, n_bank), tm)
-            pltpu.make_async_remote_copy(
-                src_ref=best, dst_ref=heard.at[bank], send_sem=best_out, recv_sem=best_in,
-                device_id=to, device_id_type=MESH,
-            ).start()
-            return carry
-
-        lax.fori_loop(1, n_bank, announce, 0)
-
+    lax.fori_loop(0, STEPS, step, 0)
+    for g in range(GROUP):
+        if SHARE * g + SHARE - 1 >= 2 * STEPS - 2:
+            pass_on(g)
+    found[mine] = parts[mine]
+    wait_bytes(found.at[pl.ds(0, GROUP - 1)], part_in)
+    plane_best[z] = jnp.max(found[...], axis=0)
+    for i in range(1, LINE):
+        send(plane_best.at[z], plane_best.at[z], line_out, line_in, along(i))
     finish_templates(peak, total, peak_ref, mean_ref)
-    wait_bytes(strain.at[pl.ds(0, others)], gather_out)
-
-    @pl.when(owner)
-    def _():
-        wait_bytes(parts.at[pl.ds(0, LAST - FIRST - 1)], part_out)
-        wait_bytes(heard.at[pl.ds(0, SEG_CHUNKS - FIRST - 1)], best_in)
-        wait_bytes(heard.at[pl.ds(0, n_bank - 1)], best_out)
-
-    @pl.when(jnp.logical_not(owner))
-    def _():
-        wait_bytes(parts, part_out)
-        wait_bytes(heard.at[pl.ds(0, SEG_CHUNKS - FIRST)], best_in)
-
-    for c in range(n_bank):
-        low, high = FIRST, LAST - SEG_CHUNKS
-        block = heard[c, 0:DET, :]
-        if c < low:
-            block = jnp.where(tm == 0, 0.0, block)
-        if c >= high:
-            block = jnp.where(tm == 1, 0.0, block)
-        loud_ref[:, LANES * c : LANES * (c + 1)] = block
+    wait_bytes(plane_best.at[pl.ds(0, LINE - 1)], line_in)
+    best[...] = jnp.max(plane_best[...], axis=0)
+    for i in range(1, PLANE):
+        to = (z * PLANE + lax.rem(xy + i, PLANE), tm)
+        send(best, heard.at[xy], best_out, best_in, to)
+    heard[xy] = best[...]
+    wait_bytes(strain.at[pl.ds(0, LINE - 1)], lines_out)
+    wait_bytes(strain.at[pl.ds(0, (GROUP - 1) * LINE)], plane_out)
+    wait_bytes(parts.at[pl.ds(0, GROUP - 1)], part_out)
+    wait_bytes(plane_best.at[pl.ds(0, LINE - 1)], line_out)
+    wait_bytes(heard.at[pl.ds(0, PLANE - 1)], best_in)
+    wait_bytes(heard.at[pl.ds(0, PLANE - 1)], best_out)
+    silent = jnp.zeros((DET, LANES), jnp.float32)
+
+    def block_of(i):
+        inside = 0 <= i < PLANE * SHARE
+        return heard[i // SHARE, i % SHARE, 0:DET, :] if inside else silent
+
+    for c in range(SEG_CHUNKS):
+        loud_ref[:, LANES * c : LANES * (c + 1)] = jnp.where(
+            tm == 0, block_of(c - FIRST), block_of(c)
+        )
 
 
 def scratch(taps, templates):
@@ -278,7 +286,7 @@
 
 VMEM = pl.BlockSpec(memory_space=pltpu.VMEM)
 SMEM = pl.BlockSpec(memory_space=pltpu.SMEM)
-VMEM_LIMIT = 32 * 1024 * 1024
+VMEM_LIMIT = 60 * 1024 * 1024
 
 
 def per_device(
@@ -290,24 +298,30 @@
     scalars = (bin_taps, bin_band, bin_window, window_start)
     if raw_strain.shape[2] == LANES and n_bank == SEG_CHUNKS and n_tm == 2:
         slots = pltpu.VMEM((CHUNKS, SLOT, LANES), jnp.float32)
+        share = (SHARE, SLOT, LANES)
         return pl.pallas_call(
-            functools.partial(linked_kernel, n_bank),
+            linked_kernel,
             out_shape=(stats, stats, jax.ShapeDtypeStruct((DET, n_bank * LANES), jnp.float32)),
-            in_specs=[SMEM] * 5 + [VMEM] * 3,
+            in_specs=[pl.BlockSpec(memory_space=pltpu.HBM)] * 8,
             out_specs=(VMEM,) * 3,
-            scratch_shapes=[pltpu.VMEM((SLOT, LANES), jnp.float32), slots]
+            scratch_shapes=[pltpu.SMEM(v.shape, jnp.int32) for v in scalars]
+            + [pltpu.SMEM((DET,), jnp.float32)]
+            + [pltpu.VMEM(v.shape, v.dtype) for v in (raw_strain, basis_filters, recon_matrix)]
+            + [slots, slots]
             + scratch(taps, templates)
             + [
-                pltpu.VMEM((LAST - FIRST, SLOT, LANES), jnp.float32),
-                slots,
-                pltpu.VMEM((SLOT, LANES), jnp.float32),
-                pltpu.VMEM((n_bank, SLOT, LANES), jnp.float32),
+                pltpu.VMEM((GROUP,) + share, jnp.float32),
+                pltpu.VMEM((GROUP,) + share, jnp.float32),
+                pltpu.VMEM((LINE,) + share, jnp.float32),
+                pltpu.VMEM(share, jnp.float32),
+                pltpu.VMEM((PLANE,) + share, jnp.float32),
+                pltpu.SemaphoreType.DMA((8,)),
             ]
-            + [pltpu.SemaphoreType.DMA] * 6,
+            + [pltpu.SemaphoreType.DMA] * 10,
             compiler_params=pltpu.CompilerParams(
                 collective_id=0, has_side_effects=True, vmem_limit_bytes=VMEM_LIMIT
             ),
-        )(*scalars, psd_scale, raw_strain, basis_filters, recon_matrix)
+        )(*scalars, psd_scale.reshape(DET), raw_strain, basis_filters, recon_matrix)
 
     scaled = raw_strain * psd_scale
     whole = lax.all_gather(scaled, "bank", axis=2, tiled=True)

time: 32.7 us -> 34 us (1.040)
  Pallas kernels: 25.6 us -> 27.9 us
  local copies, waits for them, and re-layouts: 4.14 us -> 3.27 us
    pallas_call x1, Pallas kernels: 25.6 us -> 27.9 us  [per_device(): pl.pallas_call(linked_kernel, out_shape=(stats, stats, jax.ShapeDtypeStru...]
    unnamed x14 -> x5, local copies, waits for them, and re-layouts: 4.14 us -> 3.27 us
where the time goes in v2:
time: 34 us; the launch traced here: 33.8 us
  Pallas kernels  27.9 us (82%)
  local copies, waits for them, and re-layouts  3.27 us (10%)
  between operations  2.59 us (8%)
    pallas_call x1, Pallas kernels, per_device(): pl.pallas_call(linked_kernel, out_shape=(stats, stats, jax.ShapeDtypeStru...  27.9 us
    unnamed x5, local copies, waits for them, and re-layouts  3.27 us

profile of v2, /device:TPU:0, one launch (start us, length us, event | category | flops | bytes accessed | tf_op | source)
XLA Modules:
  0.0 33.8 jit_solution(8526301962627086332)
XLA Ops:
  2.6 27.9 %shard_map.103 = (f32[3,384]{1,0:T(4,128)}, f32[3,384]{1,0:T(4,128)}, f32[3,2048]{1,0:T(4,128)}) custom-call(s32[1]{0:T(128)S(6)} %copy.14.taps_h, s32[1]{0:T(128)S(6)} %copy.15.band_h, s32[1]{0:T(128)S(6)} %copy.16.window_h, s32[8]{0:T(128)} %start_h.1, f32[3]{0:T(128)} %bitcast.1, f32[3,1,128]{2,1,0:T(1,128)} %raw_h.1, bf16[1,128,128]{2,1,0:T(8,128)(2,1)} %basis_h.1, ...), custom_call_target="tpu_custom_call" | custom-call | tf_op jit(solution)/shard_map/pallas_call | solution.py:302
  30.5 0.0 copy-start
  30.5 1.3 %copy.17 = f32[3,384]{1,0:T(4,128)} copy(f32[3,384]{1,0:T(4,128)} %get-tuple-element.6) | data formatting | bytes 9216
  31.8 0.0 copy-done
  31.8 0.6 %copy.18 = f32[3,384]{1,0:T(4,128)} copy(f32[3,384]{1,0:T(4,128)S(1)} %copy-done) | data formatting | bytes 9216
  32.4 1.4 %copy.19 = f32[3,2048]{1,0:T(4,128)} copy(f32[3,2048]{1,0:T(4,128)} %get-tuple-element.8) | data formatting | bytes 49152
Async XLA Ops:
  30.5 1.3 %copy-start = (f32[3,384]{1,0:T(4,128)S(1)}, f32[3,384]{1,0:T(4,128)}, u32[]{:S(2)}) copy-start(f32[3,384]{1,0:T(4,128)} %get-tuple-element.7) | copy-start | bytes 13828

commit v3 on v2

--- a/solution.py
+++ b/solution.py
@@ -165,9 +165,9 @@
     peak_ref, mean_ref, loud_ref,
     taps_s, band_s, window_s, start_s, scale_s, raw_ref, basis_ref, recon_ref,
     strain, ordered, smooth, octet, taps_ref, gains, peak, total, series,
-    parts, found, plane_best, best, heard,
+    parts, found, best, heard,
     fetched, lines_out, lines_in, plane_out, plane_in,
-    part_out, part_in, line_out, line_in, best_out, best_in,
+    part_out, part_in, best_out, best_in,
 ):
     bank, tm = lax.axis_index("bank"), lax.axis_index("tm")
     z, xy = bank // PLANE, lax.rem(bank, PLANE)
@@ -186,10 +186,11 @@
         ).start()
 
     barrier = pltpu.get_barrier_semaphore()
-    for i in range(1, LINE):
-        pl.semaphore_signal(barrier, inc=1, device_id=along(i), device_id_type=MESH)
-    for i in range(1, GROUP):
-        to = across(lax.rem(mine + i, GROUP))
+    for i in range(1, LINE * PLANE):
+        to = (lax.rem(bank + i, LINE * PLANE), tm)
+        pl.semaphore_signal(barrier, inc=1, device_id=to, device_id_type=MESH)
+    for i in range(PLANE):
+        to = (z * PLANE + lax.rem(xy + i, PLANE), 1 - tm)
         pl.semaphore_signal(barrier, inc=1, device_id=to, device_id_type=MESH)
     pairs = (
         (scale_h, scale_s), (raw_h, raw_ref), (taps_h, taps_s), (band_h, band_s),
@@ -203,7 +204,7 @@
     block = jnp.concatenate([raw_ref[d] * scale_s[d] for d in range(DET)], axis=0)
     here = mine * LINE + z
     strain[here] = jnp.concatenate([block, jnp.zeros((SLOT - DET, LANES), jnp.float32)], axis=0)
-    pl.semaphore_wait(barrier, LINE + GROUP - 2)
+    pl.semaphore_wait(barrier, LINE * PLANE - 1 + PLANE)
     for i in range(1, LINE):
         send(strain.at[here], strain.at[here], lines_out, lines_in, along(i))
     clear(peak, total, series)
@@ -243,27 +244,25 @@
             pass_on(g)
     found[mine] = parts[mine]
     wait_bytes(found.at[pl.ds(0, GROUP - 1)], part_in)
-    plane_best[z] = jnp.max(found[...], axis=0)
-    for i in range(1, LINE):
-        send(plane_best.at[z], plane_best.at[z], line_out, line_in, along(i))
+    best[...] = jnp.max(found[...], axis=0)
+    for i in range(1, LINE * PLANE):
+        to = (lax.rem(bank + i, LINE * PLANE), tm)
+        send(best, heard.at[bank], best_out, best_in, to)
+    heard[bank] = best[...]
     finish_templates(peak, total, peak_ref, mean_ref)
-    wait_bytes(plane_best.at[pl.ds(0, LINE - 1)], line_in)
-    best[...] = jnp.max(plane_best[...], axis=0)
-    for i in range(1, PLANE):
-        to = (z * PLANE + lax.rem(xy + i, PLANE), tm)
-        send(best, heard.at[xy], best_out, best_in, to)
-    heard[xy] = best[...]
     wait_bytes(strain.at[pl.ds(0, LINE - 1)], lines_out)
     wait_bytes(strain.at[pl.ds(0, (GROUP - 1) * LINE)], plane_out)
     wait_bytes(parts.at[pl.ds(0, GROUP - 1)], part_out)
-    wait_bytes(plane_best.at[pl.ds(0, LINE - 1)], line_out)
-    wait_bytes(heard.at[pl.ds(0, PLANE - 1)], best_in)
-    wait_bytes(heard.at[pl.ds(0, PLANE - 1)], best_out)
+    wait_bytes(heard.at[pl.ds(0, LINE * PLANE - 1)], best_in)
+    wait_bytes(heard.at[pl.ds(0, LINE * PLANE - 1)], best_out)
     silent = jnp.zeros((DET, LANES), jnp.float32)
 
     def block_of(i):
         inside = 0 <= i < PLANE * SHARE
-        return heard[i // SHARE, i % SHARE, 0:DET, :] if inside else silent
+        if not inside:
+            return silent
+        planes = [heard[PLANE * k + i // SHARE, i % SHARE, 0:DET, :] for k in range(LINE)]
+        return functools.reduce(jnp.maximum, planes)
 
     for c in range(SEG_CHUNKS):
         loud_ref[:, LANES * c : LANES * (c + 1)] = jnp.where(
@@ -301,7 +300,11 @@
         share = (SHARE, SLOT, LANES)
         return pl.pallas_call(
             linked_kernel,
-            out_shape=(stats, stats, jax.ShapeDtypeStruct((DET, n_bank * LANES), jnp.float32)),
+            out_shape=(
+                pltpu.VMEM(stats.shape, jnp.float32),
+                pltpu.VMEM(stats.shape, jnp.float32),
+                pltpu.VMEM((DET, n_bank * LANES), jnp.float32),
+            ),
             in_specs=[pl.BlockSpec(memory_space=pltpu.HBM)] * 8,
             out_specs=(VMEM,) * 3,
             scratch_shapes=[pltpu.SMEM(v.shape, jnp.int32) for v in scalars]
@@ -312,12 +315,11 @@
             + [
                 pltpu.VMEM((GROUP,) + share, jnp.float32),
                 pltpu.VMEM((GROUP,) + share, jnp.float32),
-                pltpu.VMEM((LINE,) + share, jnp.float32),
                 pltpu.VMEM(share, jnp.float32),
-                pltpu.VMEM((PLANE,) + share, jnp.float32),
+                pltpu.VMEM((LINE * PLANE,) + share, jnp.float32),
                 pltpu.SemaphoreType.DMA((8,)),
             ]
-            + [pltpu.SemaphoreType.DMA] * 10,
+            + [pltpu.SemaphoreType.DMA] * 8,
             compiler_params=pltpu.CompilerParams(
                 collective_id=0, has_side_effects=True, vmem_limit_bytes=VMEM_LIMIT
             ),

time: 34 us -> 30.2 us (0.89)
  Pallas kernels: 27.9 us -> 25.3 us
  local copies, waits for them, and re-layouts: 3.27 us -> 1.8 us
    pallas_call x1, Pallas kernels: 27.9 us -> 25.3 us  [per_device(): pl.pallas_call(linked_kernel, out_shape=(pltpu.VMEM(stats.shape, jnp.floa...]
    unnamed x5 -> x3, local copies, waits for them, and re-layouts: 3.27 us -> 1.8 us
where the time goes in v3:
time: 30.2 us; the launch traced here: 29.7 us
  Pallas kernels  25.3 us (84%)
  between operations  2.58 us (9%)
  local copies, waits for them, and re-layouts  1.8 us (6%)
    pallas_call x1, Pallas kernels, per_device(): pl.pallas_call(linked_kernel, out_shape=(pltpu.VMEM(stats.shape, jnp.floa...  25.3 us
    unnamed x3, local copies, waits for them, and re-layouts  1.8 us

profile of v3, /device:TPU:0, one launch (start us, length us, event | category | flops | bytes accessed | tf_op | source)
XLA Modules:
  0.0 29.7 jit_solution(7854883681686010165)
XLA Ops:
  2.6 25.3 %shard_map.103 = (f32[3,384]{1,0:T(4,128)S(1)}, f32[3,384]{1,0:T(4,128)S(1)}, f32[3,2048]{1,0:T(4,128)S(1)}) custom-call(s32[1]{0:T(128)S(6)} %copy.17.taps_h, s32[1]{0:T(128)S(6)} %copy.18.band_h, s32[1]{0:T(128)S(6)} %copy.19.window_h, s32[8]{0:T(128)} %start_h.1, f32[3]{0:T(128)} %bitcast.1, f32[3,1,128]{2,1,0:T(1,128)} %raw_h.1, ...), custom_call_target="tpu_custom_call" | custom-call | tf_op jit(solution)/shard_map/pallas_call | solution.py:301
  27.9 0.6 %copy.14 = f32[3,384]{1,0:T(4,128)} copy(f32[3,384]{1,0:T(4,128)S(1)} %get-tuple-element.3) | data formatting | bytes 9216
  28.5 0.6 %copy.15 = f32[3,384]{1,0:T(4,128)} copy(f32[3,384]{1,0:T(4,128)S(1)} %get-tuple-element.4) | data formatting | bytes 9216
  29.1 0.6 %copy.16 = f32[3,2048]{1,0:T(4,128)} copy(f32[3,2048]{1,0:T(4,128)S(1)} %get-tuple-element.5) | data formatting | bytes 49152

commit v4 on v3

--- a/solution.py
+++ b/solution.py
@@ -223,8 +223,9 @@
     lay_all(ordered, rate, start, offset, smooth, octet, taps_ref)
 
     def pass_on(g):
-        for i in range(SHARE):
-            parts[g, i] = series[PAD + FIRST + SHARE * g + i - start]
+        rows = [series[PAD + FIRST + SHARE * g + i - start] for i in range(SHARE)]
+        rows.append(jnp.zeros((SLOT, LANES), jnp.float32))
+        parts[g] = jnp.concatenate(rows, axis=0).astype(jnp.bfloat16)
 
         @pl.when(mine != g)
         def _():
@@ -244,7 +245,7 @@
             pass_on(g)
     found[mine] = parts[mine]
     wait_bytes(found.at[pl.ds(0, GROUP - 1)], part_in)
-    best[...] = jnp.max(found[...], axis=0)
+    best[...] = jnp.max(found[...].astype(jnp.float32), axis=0).astype(jnp.bfloat16)
     for i in range(1, LINE * PLANE):
         to = (lax.rem(bank + i, LINE * PLANE), tm)
         send(best, heard.at[bank], best_out, best_in, to)
@@ -257,12 +258,19 @@
     wait_bytes(heard.at[pl.ds(0, LINE * PLANE - 1)], best_out)
     silent = jnp.zeros((DET, LANES), jnp.float32)
 
+    merged = [
+        functools.reduce(
+            jnp.maximum, [heard[PLANE * k + j].astype(jnp.float32) for k in range(LINE)]
+        )
+        for j in range(PLANE)
+    ]
+
     def block_of(i):
         inside = 0 <= i < PLANE * SHARE
         if not inside:
             return silent
-        planes = [heard[PLANE * k + i // SHARE, i % SHARE, 0:DET, :] for k in range(LINE)]
-        return functools.reduce(jnp.maximum, planes)
+        at = SLOT * (i % SHARE)
+        return merged[i // SHARE][at : at + DET, :]
 
     for c in range(SEG_CHUNKS):
         loud_ref[:, LANES * c : LANES * (c + 1)] = jnp.where(
@@ -297,7 +305,7 @@
     scalars = (bin_taps, bin_band, bin_window, window_start)
     if raw_strain.shape[2] == LANES and n_bank == SEG_CHUNKS and n_tm == 2:
         slots = pltpu.VMEM((CHUNKS, SLOT, LANES), jnp.float32)
-        share = (SHARE, SLOT, LANES)
+        share = (SHARE * SLOT + SLOT, LANES)
         return pl.pallas_call(
             linked_kernel,
             out_shape=(
@@ -313,10 +321,10 @@
             + [slots, slots]
             + scratch(taps, templates)
             + [
-                pltpu.VMEM((GROUP,) + share, jnp.float32),
-                pltpu.VMEM((GROUP,) + share, jnp.float32),
-                pltpu.VMEM(share, jnp.float32),
-                pltpu.VMEM((LINE * PLANE,) + share, jnp.float32),
+                pltpu.VMEM((GROUP,) + share, jnp.bfloat16),
+                pltpu.VMEM((GROUP,) + share, jnp.bfloat16),
+                pltpu.VMEM(share, jnp.bfloat16),
+                pltpu.VMEM((LINE * PLANE,) + share, jnp.bfloat16),
                 pltpu.SemaphoreType.DMA((8,)),
             ]
             + [pltpu.SemaphoreType.DMA] * 8,

time: 30.2 us -> 30.1 us (level)
  no operation moved by 1% of the time
where the time goes in v4:
time: 30.1 us; the launch traced here: 29.6 us
  Pallas kernels  25.3 us (84%)
  between operations  2.58 us (9%)
  local copies, waits for them, and re-layouts  1.8 us (6%)
    pallas_call x1, Pallas kernels, per_device(): pl.pallas_call(linked_kernel, out_shape=(pltpu.VMEM(stats.shape, jnp.floa...  25.3 us
    unnamed x3, local copies, waits for them, and re-layouts  1.8 us

profile of v4, /device:TPU:0, one launch (start us, length us, event | category | flops | bytes accessed | tf_op | source)
XLA Modules:
  0.0 29.6 jit_solution(9944264455076085733)
XLA Ops:
  2.6 25.3 %shard_map.103 = (f32[3,384]{1,0:T(4,128)S(1)}, f32[3,384]{1,0:T(4,128)S(1)}, f32[3,2048]{1,0:T(4,128)S(1)}) custom-call(s32[1]{0:T(128)S(6)} %copy.17.taps_h, s32[1]{0:T(128)S(6)} %copy.18.band_h, s32[1]{0:T(128)S(6)} %copy.19.window_h, s32[8]{0:T(128)} %start_h.1, f32[3]{0:T(128)} %bitcast.1, f32[3,1,128]{2,1,0:T(1,128)} %raw_h.1, ...), custom_call_target="tpu_custom_call" | custom-call | tf_op jit(solution)/shard_map/pallas_call | solution.py:309
  27.8 0.6 %copy.14 = f32[3,384]{1,0:T(4,128)} copy(f32[3,384]{1,0:T(4,128)S(1)} %get-tuple-element.3) | data formatting | bytes 9216
  28.4 0.6 %copy.15 = f32[3,384]{1,0:T(4,128)} copy(f32[3,384]{1,0:T(4,128)S(1)} %get-tuple-element.4) | data formatting | bytes 9216
  29.0 0.6 %copy.16 = f32[3,2048]{1,0:T(4,128)} copy(f32[3,2048]{1,0:T(4,128)S(1)} %get-tuple-element.5) | data formatting | bytes 49152
